TPU v7x, 512 devices: a whole 4x4x16 slice. The times are simulated.
512 devices in a mesh: row: 64 (over x, z), col: 8 (over y, core).
Axes of the slice: x: 4, y: 4, z: 16, core: 2. Of those that a mesh axis runs over, the one named last changes fastest.
Arguments:
- kelvin_start: float32 [512, 512, 128], P('row', 'col'), may hold values from 1 to 2.5
- mass_ratio: float32 [512, 512, 128], P('row', 'col'), may hold values from 0.6 to 1
- material_region_labels: int32 [512, 512], P('row', 'col'), may hold values from 0 to 7
- pristine_conductivity: float32 [8], replicated, may hold values from 0.5 to 2
- burnt_conductivity: float32 [8], replicated, may hold values from 0.5 to 2
- burnt_mass_ratio: float32 [8], replicated, may hold values from 0.25 to 0.5
- arrhenius_prefactor: float32 [8], replicated, may hold values from 1 to 30
- onset_kelvin: float32 [8], replicated, may hold values from 2 to 6
- exchange_film_strength: float32 [64, 8, 64, 128], P('row', 'col'), may hold values from 0.25 to 4
- stagnation_kelvin: float32 [64, 8, 64, 128], P('row', 'col'), may hold values from 2 to 6
- receiving_element: int32 [64, 8, 64, 128], P('row', 'col'), may hold values from 0 to 511
- occupied_slot_totals: int32 [64, 8, 64], P('row', 'col'), may hold values from 16 to 128, as said below
Outputs:
- kelvin_after: float32 [512, 512, 128], P('row', 'col')
- mass_ratio_after: float32 [512, 512, 128], P('row', 'col')
Inputs may be any that keep to these rules, and one draw needn't show every extreme that they name: `occupied_slot_totals`: live slots come first in each block; in every col one destination tile receives 128 live faces from every source; slots at or past the count hold arbitrary values. `receiving_element`: cell i * 64 + j is row i and column j of the destination tile.
All inputs are finite; a program needn't handle non-finite values.
Results may differ from a plain program's by a relative error of at most 0.0003.
Values sent between devices are 32-bit elements; how exact they have to be, the bound alone decides.
A program may use at most 64 MiB of HBM per device.

v0:
```python
import jax
import jax.numpy as jnp
from jax import lax
from jax.sharding import PartitionSpec as P

R_X = 32
R_Y = 64
R_Z = 1024
EXTERIOR_SHARE = 16
HEAT_OF_PYROLYSIS = 0.3


def take_part(values, first_index, end_index, stride, solve_dim):
    return lax.slice_in_dim(values, first_index, end_index, stride, solve_dim)


def extend_end(values, filler, solve_dim):
    new_shape = list(values.shape)
    new_shape[solve_dim] = 1
    return jnp.concatenate([values, jnp.full(new_shape, filler, values.dtype)], solve_dim)


def merge_halves(even_value, odd_value, odd_count, solve_dim):
    even_head = take_part(even_value, 0, odd_count, 1, solve_dim)
    paired = jnp.stack([even_head, odd_value], solve_dim + 1)
    new_shape = list(even_head.shape)
    new_shape[solve_dim] = 2 * odd_count
    merged = paired.reshape(new_shape)
    return merged


def cyclic_solve(sub_diag, main_diag, super_diag, rights, solve_dim):
    length = main_diag.shape[solve_dim]
    if length == 1:
        return [vector / main_diag for vector in rights]
    odd_count = length // 2
    even_count = length - odd_count
    even_parts = [
        take_part(operand, 0, length, 2, solve_dim) for operand in (sub_diag, main_diag, super_diag)
    ]
    odd_parts = [
        take_part(operand, 1, length, 2, solve_dim) for operand in (sub_diag, main_diag, super_diag)
    ]
    even_rights = [take_part(vector, 0, length, 2, solve_dim) for vector in rights]
    odd_rights = [take_part(vector, 1, length, 2, solve_dim) for vector in rights]
    left_sub, left_main, left_super = [
        take_part(operand, 0, odd_count, 1, solve_dim) for operand in even_parts
    ]
    left_rights = [take_part(vector, 0, odd_count, 1, solve_dim) for vector in even_rights]
    right_sub = take_part(extend_end(even_parts[0], 0.0, solve_dim), 1, odd_count + 1, 1, solve_dim)
    right_main = take_part(
        extend_end(even_parts[1], 1.0, solve_dim), 1, odd_count + 1, 1, solve_dim
    )
    right_super = take_part(
        extend_end(even_parts[2], 0.0, solve_dim), 1, odd_count + 1, 1, solve_dim
    )
    right_rights = [
        take_part(extend_end(vector, 0.0, solve_dim), 1, odd_count + 1, 1, solve_dim)
        for vector in even_rights
    ]
    left_factor = -odd_parts[0] / left_main
    right_factor = -odd_parts[2] / right_main
    reduced_sub = left_factor * left_sub
    reduced_main = odd_parts[1] + left_factor * left_super + right_factor * right_sub
    reduced_super = right_factor * right_super
    reduced_rights = [
        odd_part + left_factor * left_part + right_factor * right_part
        for odd_part, left_part, right_part in zip(odd_rights, left_rights, right_rights)
    ]
    odd_solutions = cyclic_solve(
        reduced_sub, reduced_main, reduced_super, reduced_rights, solve_dim
    )
    results = []
    for even_part, odd_part in zip(even_rights, odd_solutions):
        edge_shape = list(odd_part.shape)
        edge_shape[solve_dim] = 1
        zero_plane = jnp.zeros(edge_shape, odd_part.dtype)
        padded = jnp.concatenate([zero_plane, odd_part, zero_plane], solve_dim)
        before = take_part(padded, 0, even_count, 1, solve_dim)
        after_vals = take_part(padded, 1, even_count + 1, 1, solve_dim)
        even_value = (even_part - even_parts[0] * before - even_parts[2] * after_vals) / even_parts[
            1
        ]
        results.append(merge_halves(even_value, odd_part, odd_count, solve_dim))
    return results


def sweep_coefficients(capacity, diffuse_thermal_energy, diffusion, solve_dim):
    length = diffuse_thermal_energy.shape[solve_dim]
    face_cond = 0.5 * (
        take_part(diffuse_thermal_energy, 0, length - 1, 1, solve_dim)
        + take_part(diffuse_thermal_energy, 1, length, 1, solve_dim)
    )
    edge_shape = list(diffuse_thermal_energy.shape)
    edge_shape[solve_dim] = 1
    zero_edge = jnp.zeros(edge_shape, diffuse_thermal_energy.dtype)
    sub_diag = -diffusion * jnp.concatenate([zero_edge, face_cond], solve_dim)
    super_diag = -diffusion * jnp.concatenate([face_cond, zero_edge], solve_dim)
    main_diag = capacity - sub_diag - super_diag
    return (sub_diag, main_diag, super_diag)


def solve_lines(pieces, diffusion, solve_dim):
    sub_diag, main_diag, super_diag = sweep_coefficients(pieces[1], pieces[2], diffusion, solve_dim)
    return cyclic_solve(sub_diag, main_diag, super_diag, [pieces[0]], solve_dim)[0]


def column_values(material_region_labels, property_arrays):
    matches = (
        material_region_labels[..., None]
        == jnp.arange(property_arrays[0].shape[0], dtype=jnp.int32)
    ).astype(jnp.float32)
    return [jnp.sum(matches * lookup, axis=-1)[..., None] for lookup in property_arrays]


def decompose_through_layers(
    kelvin_start,
    mass_ratio,
    material_region_labels,
    property_arrays,
    exterior_multiplier,
    exterior_flux_amount,
):
    virgin, charred, residue, rate_col, energy = column_values(
        material_region_labels, property_arrays
    )
    old_conduct = charred + (virgin - charred) * (mass_ratio - residue) / (1.0 - residue)
    thickness_dimension = kelvin_start.ndim - 1
    sub_diag, main_diag, super_diag = sweep_coefficients(
        mass_ratio, old_conduct, float(R_Z), thickness_dimension
    )
    main_diag = main_diag.at[..., 0].add(float(EXTERIOR_SHARE) * exterior_multiplier)
    forcing_vector = (
        (mass_ratio * kelvin_start).at[..., 0].add(float(EXTERIOR_SHARE) * exterior_flux_amount)
    )
    depth_temp = cyclic_solve(
        sub_diag, main_diag, super_diag, [forcing_vector], thickness_dimension
    )[0]
    extent = rate_col * jnp.exp(-energy / depth_temp)
    mass_ratio_after = residue + (mass_ratio - residue) * jnp.exp(-extent)
    warmed_fields = (
        depth_temp - HEAT_OF_PYROLYSIS * (mass_ratio - mass_ratio_after) / mass_ratio_after
    )
    diffuse_thermal_energy = charred + (virgin - charred) * (mass_ratio_after - residue) / (
        1.0 - residue
    )
    return (warmed_fields, mass_ratio_after, diffuse_thermal_energy)


def solve_x(pieces):
    return solve_lines(pieces, float(R_X), 0)


def sweep_trailing_lines(pieces):
    return solve_lines(pieces, float(R_Y), 1)


def per_device(
    kelvin_start,
    mass_ratio,
    material_region_labels,
    pristine_conductivity,
    burnt_conductivity,
    burnt_mass_ratio,
    arrhenius_prefactor,
    onset_kelvin,
    exchange_film_strength,
    stagnation_kelvin,
    receiving_element,
    occupied_slot_totals,
):
    patch_leading_extent, patch_trailing_extent, layer_number = kelvin_start.shape
    sources = lax.axis_size("row")
    cell_count = patch_leading_extent * patch_trailing_extent
    slot_index = jnp.arange(exchange_film_strength.shape[-1], dtype=jnp.int32)
    live_slots = (slot_index < occupied_slot_totals[..., None]).astype(jnp.float32)
    blending_shares = (exchange_film_strength * live_slots)[0, 0]
    flux_arriving = blending_shares * stagnation_kelvin[0, 0]
    targets = receiving_element[0, 0]
    offsets = jnp.arange(sources, dtype=jnp.int32)[:, None] * cell_count + targets
    flat_ids = offsets.reshape(-1)
    tile_weight = jax.ops.segment_sum(
        blending_shares.reshape(-1), flat_ids, num_segments=sources * cell_count
    )
    tile_heat = jax.ops.segment_sum(
        flux_arriving.reshape(-1), flat_ids, num_segments=sources * cell_count
    )
    exterior_multiplier, exterior_flux_amount = (
        lax.psum_scatter(tile_weight, "row", scatter_dimension=0, tiled=True),
        lax.psum_scatter(tile_heat, "row", scatter_dimension=0, tiled=True),
    )
    exterior_multiplier = exterior_multiplier.reshape(patch_leading_extent, patch_trailing_extent)
    exterior_flux_amount = exterior_flux_amount.reshape(patch_leading_extent, patch_trailing_extent)
    property_arrays = (
        pristine_conductivity,
        burnt_conductivity,
        burnt_mass_ratio,
        arrhenius_prefactor,
        onset_kelvin,
    )
    warmed_fields, mass_ratio_after, diffuse_thermal_energy = decompose_through_layers(
        kelvin_start,
        mass_ratio,
        material_region_labels,
        property_arrays,
        exterior_multiplier,
        exterior_flux_amount,
    )
    forcing_vector = mass_ratio_after * warmed_fields
    line_share = patch_trailing_extent * layer_number // sources
    flat_parts = (forcing_vector, mass_ratio_after, diffuse_thermal_energy)
    solved_x = solve_x(
        (
            lax.all_to_all(flat_parts[0], "row", split_axis=1, concat_axis=0, tiled=True),
            lax.all_to_all(flat_parts[1], "row", split_axis=1, concat_axis=0, tiled=True),
            lax.all_to_all(flat_parts[2], "row", split_axis=1, concat_axis=0, tiled=True),
        )
    )
    across = lax.all_to_all(solved_x, "row", split_axis=0, concat_axis=1, tiled=True)
    forcing_vector_other = mass_ratio_after * across
    solved_state = sweep_trailing_lines(
        (
            lax.all_to_all(forcing_vector_other, "col", split_axis=0, concat_axis=1, tiled=True),
            lax.all_to_all(mass_ratio_after, "col", split_axis=0, concat_axis=1, tiled=True),
            lax.all_to_all(diffuse_thermal_energy, "col", split_axis=0, concat_axis=1, tiled=True),
        )
    )
    kelvin_after = lax.all_to_all(solved_state, "col", split_axis=1, concat_axis=0, tiled=True)
    return (kelvin_after, mass_ratio_after)


def solution(mesh):
    return jax.shard_map(
        per_device,
        mesh=mesh,
        in_specs=(
            P("row", "col", None),
            P("row", "col", None),
            P("row", "col"),
            P(),
            P(),
            P(),
            P(),
            P(),
            P("row", "col", None, None),
            P("row", "col", None, None),
            P("row", "col", None, None),
            P("row", "col", None),
        ),
        out_specs=(P("row", "col", None), P("row", "col", None)),
        check_vma=False,
    )
```

profile of v0, /device:TPU:1, one launch (start us, length us, event | category | flops | bytes accessed | tf_op | source)
XLA Modules:
  0.0 658.0 jit_solution(1565937443796117026)
XLA Ops:
  8.8 57.7 %scatter_custom_fusion = f32[32768]{0:T(1024)} fusion(s32[8192]{0:T(1024)S(1)} %bitcast.253, f32[8192]{0:T(1024)S(1)} %get-tuple-element.52, f32[]{:T(128)} %constant.67.clone.1), kind=kCustom, calls=%fused_computation.156 | custom fusion | flops 8192 | bytes 131076 | tf_op jit(solution)/shard_map/scatter-add | solution.py:185
  66.5 57.6 %scatter_custom_fusion.1 = f32[32768]{0:T(1024)} fusion(s32[8192]{0:T(1024)S(1)} %bitcast.254, f32[8192]{0:T(1024)S(1)} %get-tuple-element.53, f32[]{:T(128)} %constant.67.clone.1), kind=kCustom, calls=%fused_computation.154 | custom fusion | flops 8192 | bytes 131076 | tf_op jit(solution)/shard_map/scatter-add | solution.py:182
  125.6 4.5 slice.1033
  130.1 4.5 slice.1025
  134.7 4.5 slice.1020
  139.2 4.5 slice.1022
  145.8 236.7 %all-reduce.121.cloned.1.call-done = (f32[32768]{0:T(1024)}, f32[32768]{0:T(1024)}) async-done(((f32[32768]{0:T(1024)}, f32[32768]{0:T(1024)}), (f32[32768]{0:T(1024)}, f32[32768]{0:T(1024)})) %all-reduce.121.cloned.1.call-update) | async-done | bytes 262160
  383.9 4.5 slice.1017
  388.4 4.5 slice.1021
  393.4 4.5 slice.1024
  397.9 4.5 slice.1032
  405.3 3.0 slice.1030
  410.6 3.0 slice.1044
  415.9 3.0 slice.1031
  421.2 3.0 slice.1037
  453.9 2.7 multiply_add_fusion.6
  465.1 2.5 multiply_add_fusion.4
  495.9 8.0 %all-to-all-start = ((f32[8,64,128]{2,0,1:T(8,128)}), f32[8,64,128]{2,0,1:T(8,128)S(1)}, u32[]{:S(2)}, u32[]{:S(2)}) async-start(f32[8,64,128]{2,0,1:T(8,128)} %copy.540), calls=%async_computation | async-start | bytes 524288 | tf_op jit(solution)/shard_map/all_to_all | solution.py:214
  507.7 11.8 %all-to-all-done = f32[8,64,128]{2,0,1:T(8,128)S(1)} async-done(((f32[8,64,128]{2,0,1:T(8,128)}), f32[8,64,128]{2,0,1:T(8,128)S(1)}, u32[]{:S(2)}, u32[]{:S(2)}) %all-to-all-start) | async-done | bytes 262176 | tf_op jit(solution)/shard_map/all_to_all | solution.py:214
  519.5 6.2 all-to-all-start.1
  527.5 13.6 %all-to-all-done.1 = f32[8,64,128]{2,0,1:T(8,128)S(1)} async-done(((f32[8,64,128]{2,0,1:T(8,128)}), f32[8,64,128]{2,0,1:T(8,128)S(1)}, u32[]{:S(2)}, u32[]{:S(2)}) %all-to-all-start.1) | async-done | bytes 262176 | tf_op jit(solution)/shard_map/all_to_all | solution.py:216
  541.2 6.4 all-to-all-start.2
  547.8 15.2 %all-to-all-done.2 = f32[8,64,128]{2,0,1:T(8,128)S(1)} async-done(((f32[8,64,128]{2,0,1:T(8,128)}), f32[8,64,128]{2,0,1:T(8,128)S(1)}, u32[]{:S(2)}, u32[]{:S(2)}) %all-to-all-start.2) | async-done | bytes 262176 | tf_op jit(solution)/shard_map/all_to_all | solution.py:215
  563.0 19.4 %all-to-all-start.5 = ((f32[8,64,128]{2,1,0:T(8,128)}), f32[8,64,128]{2,1,0:T(8,128)S(1)}, u32[]{:S(2)}, u32[]{:S(2)}) async-start(f32[8,64,128]{2,1,0:T(8,128)} %divide_add_fusion), calls=%async_computation.5 | async-start | bytes 524288 | tf_op jit(solution)/shard_map/all_to_all | solution.py:225
  585.9 3.0 all-to-all-done.5
  588.9 6.3 all-to-all-start.3
  595.3 18.6 %all-to-all-done.3 = f32[512,1,128]{2,1,0:T(1,128)S(1)} async-done(((f32[512,1,128]{2,1,0:T(1,128)}), f32[512,1,128]{2,1,0:T(1,128)S(1)}, u32[]{:S(2)}, u32[]{:S(2)}) %all-to-all-start.3) | async-done | bytes 262176 | tf_op jit(solution)/shard_map/all_to_all | solution.py:219
  613.9 6.7 %all-to-all-start.6 = ((f32[8,64,128]{2,1,0:T(8,128)}), f32[8,64,128]{2,1,0:T(8,128)S(1)}, u32[]{:S(2)}, u32[]{:S(2)}) async-start(f32[8,64,128]{2,1,0:T(8,128)} %get-tuple-element.163), calls=%async_computation.6 | async-start | bytes 524288 | tf_op jit(solution)/shard_map/all_to_all | solution.py:224
  622.3 4.8 all-to-all-done.6
  627.1 4.4 all-to-all-start.4
  632.1 5.9 all-to-all-done.4
  640.3 9.9 %all_to_all.120 = f32[1,512,128]{2,0,1:T(1,128)S(1)} all-to-all(f32[1,512,128]{2,0,1:T(1,128)S(1)} %bitcast.222), channel_id=1, replica_groups=mesh['row'=64,'col'=8] {'col'}, dimensions={1} | all-to-all | bytes 524288 | tf_op jit(solution)/shard_map/all_to_all | solution.py:228
  (355 shorter events, 95.9 us)
Async XLA Ops:
  7.2 0.8 copy-start.16
  7.2 375.3 %all-reduce.121.cloned.1.call-start = ((), (), s32[]{:S(2)}) async-start(), calls=%async_computation.8 | async-start | bytes 524288
  7.9 0.8 copy-start.17
  7.9 0.8 copy-start.18
  8.0 0.7 copy-start.20
  8.8 116.2 %copy-start.11 = (f32[8,64,128]{2,1,0:T(8,128)S(1)}, f32[8,64,128]{2,1,0:T(8,128)}, u32[]{:S(2)}) copy-start(f32[8,64,128]{2,1,0:T(8,128)} %param.17) | copy-start | bytes 786436
  8.8 116.2 %copy-start.15 = (f32[8,64,128]{2,1,0:T(8,128)S(1)}, f32[8,64,128]{2,1,0:T(8,128)}, u32[]{:S(2)}) copy-start(f32[8,64,128]{2,1,0:T(8,128)} %param.16) | copy-start | bytes 786436
  124.1 0.7 copy-start.22
  124.1 0.7 copy-start.23
  124.1 0.7 copy-start.24
  124.1 0.7 copy-start.25
  472.9 1.1 copy-start.9
  476.4 1.0 copy-start.10
  479.3 2.0 copy-start.7
  479.3 2.0 copy-start.8
  481.3 4.1 copy-start.5
  481.3 4.1 copy-start.6
  483.4 2.0 copy-start.3
  483.4 2.0 copy-start.4
  487.3 0.9 copy-start.13
  488.3 1.0 copy-start.1
  488.3 1.0 copy-start.2
  488.5 1.0 copy-start
  490.4 0.9 copy-start.14
  493.1 1.0 copy-start.12
  495.9 23.6 %all-to-all-start = ((f32[8,64,128]{2,0,1:T(8,128)}), f32[8,64,128]{2,0,1:T(8,128)S(1)}, u32[]{:S(2)}, u32[]{:S(2)}) async-start(f32[8,64,128]{2,0,1:T(8,128)} %copy.540), calls=%async_computation | async-start | bytes 524288 | tf_op jit(solution)/shard_map/all_to_all | solution.py:214
  519.5 21.7 %all-to-all-start.1 = ((f32[8,64,128]{2,0,1:T(8,128)}), f32[8,64,128]{2,0,1:T(8,128)S(1)}, u32[]{:S(2)}, u32[]{:S(2)}) async-start(f32[8,64,128]{2,0,1:T(8,128)} %copy.541), calls=%async_computation.1 | async-start | bytes 524288 | tf_op jit(solution)/shard_map/all_to_all | solution.py:216
  541.2 21.8 %all-to-all-start.2 = ((f32[8,64,128]{2,0,1:T(8,128)}), f32[8,64,128]{2,0,1:T(8,128)S(1)}, u32[]{:S(2)}, u32[]{:S(2)}) async-start(f32[8,64,128]{2,0,1:T(8,128)} %copy.542), calls=%async_computation.2 | async-start | bytes 524288 | tf_op jit(solution)/shard_map/all_to_all | solution.py:215
  563.0 25.9 %all-to-all-start.5 = ((f32[8,64,128]{2,1,0:T(8,128)}), f32[8,64,128]{2,1,0:T(8,128)S(1)}, u32[]{:S(2)}, u32[]{:S(2)}) async-start(f32[8,64,128]{2,1,0:T(8,128)} %divide_add_fusion), calls=%async_computation.5 | async-start | bytes 524288 | tf_op jit(solution)/shard_map/all_to_all | solution.py:225
  588.9 25.0 %all-to-all-start.3 = ((f32[512,1,128]{2,1,0:T(1,128)}), f32[512,1,128]{2,1,0:T(1,128)S(1)}, u32[]{:S(2)}, u32[]{:S(2)}) async-start(f32[512,1,128]{2,1,0:T(1,128)} %bitcast.85), calls=%async_computation.3 | async-start | bytes 524288 | tf_op jit(solution)/shard_map/all_to_all | solution.py:219
  613.9 13.2 %all-to-all-start.6 = ((f32[8,64,128]{2,1,0:T(8,128)}), f32[8,64,128]{2,1,0:T(8,128)S(1)}, u32[]{:S(2)}, u32[]{:S(2)}) async-start(f32[8,64,128]{2,1,0:T(8,128)} %get-tuple-element.163), calls=%async_computation.6 | async-start | bytes 524288 | tf_op jit(solution)/shard_map/all_to_all | solution.py:224
  627.1 10.9 %all-to-all-start.4 = ((f32[8,64,128]{2,1,0:T(8,128)}), f32[8,64,128]{2,1,0:T(8,128)S(1)}, u32[]{:S(2)}, u32[]{:S(2)}) async-start(f32[8,64,128]{2,1,0:T(8,128)} %bitcast_multiply_fusion), calls=%async_computation.4 | async-start | bytes 524288 | tf_op jit(solution)/shard_map/all_to_all | solution.py:223
  (2 other events, 1.4 us)
Sparse Core Ops, SparseCore 0:
  124.3 258.1 all-reduce.120
where the time goes:
time: 667 us; the launch traced here: 658 us
  waiting for transfers between devices  310 us (46%)
  other arithmetic  142 us (21%)
  local copies, waits for them, and re-layouts  122 us (18%)
  starting transfers between devices  57.4 us (9%)
  between operations  16.5 us (2%)
  blocking collectives  9.95 us (1%)
    unnamed x2, waiting for transfers between devices  237 us
    slice x177, local copies, waits for them, and re-layouts, take_part(): return lax.slice_in_dim(values, first_index, end_index, stride, solve_dim)  101 us
    scatter-add x1, other arithmetic, per_device(): jax.ops.segment_sum(flux_arriving.reshape(-1), flat_ids, num_segments=sou...  57.7 us
    scatter-add x1, other arithmetic, per_device(): jax.ops.segment_sum(blending_shares.reshape(-1), flat_ids, num_segments=s...  57.6 us
    all_to_all x1, starting transfers between devices, per_device(): lax.all_to_all(diffuse_thermal_energy, 'col', split_axis=0, concat_axis=1...  19.4 us
    all_to_all x1, waiting for transfers between devices, per_device(): lax.all_to_all(solved_x, 'row', split_axis=0, concat_axis=1, tiled=True)  18.6 us
    all_to_all x1, waiting for transfers between devices, per_device(): lax.all_to_all(flat_parts[1], 'row', split_axis=1, concat_axis=0, tiled=T...  15.2 us
    all_to_all x1, waiting for transfers between devices, per_device(): lax.all_to_all(flat_parts[2], 'row', split_axis=1, concat_axis=0, tiled=T...  13.6 us
  transfers between devices with their start and end apart: 8, of which 8 were waited for; matrix products, arithmetic and copies ran while one was open for 5% of the time, Pallas kernels for 0%

commit v1 on v0

--- a/solution.py
+++ b/solution.py
@@ -8,6 +8,22 @@
 R_Z = 1024
 EXTERIOR_SHARE = 16
 HEAT_OF_PYROLYSIS = 0.3
+
+
+def swapped_with_each(shard, axis, split, join):
+    ways, here = (lax.axis_size(axis), lax.axis_index(axis))
+    width = shard.shape[split] // ways
+    shape = list(shard.shape)
+    shape[split] = width
+    height = shape[join]
+    shape[join] = height * ways
+    full = jnp.zeros(shape, shard.dtype)
+    for mask in range(ways):
+        part = lax.dynamic_slice_in_dim(shard, (here ^ mask) * width, width, axis=split)
+        if mask:
+            part = lax.ppermute(part, axis, [(d, d ^ mask) for d in range(ways)])
+        full = lax.dynamic_update_slice_in_dim(full, part, (here ^ mask) * height, axis=join)
+    return full
 
 
 def take_part(values, first_index, end_index, stride, solve_dim):
@@ -222,7 +238,7 @@
         (
             lax.all_to_all(forcing_vector_other, "col", split_axis=0, concat_axis=1, tiled=True),
             lax.all_to_all(mass_ratio_after, "col", split_axis=0, concat_axis=1, tiled=True),
-            lax.all_to_all(diffuse_thermal_energy, "col", split_axis=0, concat_axis=1, tiled=True),
+            swapped_with_each(diffuse_thermal_energy, "col", 0, 1),
         )
     )
     kelvin_after = lax.all_to_all(solved_state, "col", split_axis=1, concat_axis=0, tiled=True)

time: 667 us -> 664 us (level)
  waiting for transfers between devices: 310 us -> 279 us
  starting transfers between devices: 57.4 us -> 85.3 us
    ppermute x0 -> x7, starting transfers between devices: none -> 40.8 us  [swapped_with_each(): part = lax.ppermute(part, axis, [(d, d ^ mask) for d in range(ways)])]
    all_to_all x1 -> x0, starting transfers between devices: 19.4 us -> none  [per_device(): lax.all_to_all(diffuse_thermal_energy, 'col', split_axis=0, concat_axis=1...]
    all_to_all x1, waiting for transfers between devices: 18.6 us -> 0.01 us  [per_device(): lax.all_to_all(solved_x, 'row', split_axis=0, concat_axis=1, tiled=True)]
    all_to_all x1, waiting for transfers between devices: 11.8 us -> 0.01 us  [per_device(): lax.all_to_all(flat_parts[0], 'row', split_axis=1, concat_axis=0, tiled=T...]
    all_to_all x1, starting transfers between devices: 6.35 us -> 14.8 us  [per_device(): lax.all_to_all(solved_x, 'row', split_axis=0, concat_axis=1, tiled=True)]
  transfers between devices with their start and end apart: 8 -> 14, of which waited for: 8 -> 6; matrix products, arithmetic and copies ran while one was open for 5% -> 4% of each run, Pallas kernels for 0% -> 0%
where the time goes in v1:
time: 664 us; the launch traced here: 654 us
  waiting for transfers between devices  279 us (42%)
  other arithmetic  142 us (21%)
  local copies, waits for them, and re-layouts  121 us (18%)
  starting transfers between devices  85.3 us (13%)
  between operations  16.8 us (3%)
  blocking collectives  9.95 us (1%)
    unnamed x2, waiting for transfers between devices  237 us
    slice x177, local copies, waits for them, and re-layouts, take_part(): return lax.slice_in_dim(values, first_index, end_index, stride, solve_dim)  101 us
    scatter-add x1, other arithmetic, per_device(): jax.ops.segment_sum(flux_arriving.reshape(-1), flat_ids, num_segments=sou...  57.7 us
    scatter-add x1, other arithmetic, per_device(): jax.ops.segment_sum(blending_shares.reshape(-1), flat_ids, num_segments=s...  57.6 us
    ppermute x7, starting transfers between devices, swapped_with_each(): part = lax.ppermute(part, axis, [(d, d ^ mask) for d in range(ways)])  40.8 us
    all_to_all x1, starting transfers between devices, per_device(): lax.all_to_all(solved_x, 'row', split_axis=0, concat_axis=1, tiled=True)  14.8 us
    all_to_all x1, waiting for transfers between devices, per_device(): lax.all_to_all(flat_parts[1], 'row', split_axis=1, concat_axis=0, tiled=T...  14.6 us
    all_to_all x1, waiting for transfers between devices, per_device(): lax.all_to_all(flat_parts[2], 'row', split_axis=1, concat_axis=0, tiled=T...  13.8 us
  transfers between devices with their start and end apart: 14, of which 6 were waited for; matrix products, arithmetic and copies ran while one was open for 4% of the time, Pallas kernels for 0%

profile of v1, /device:TPU:1, one launch (start us, length us, event | category | flops | bytes accessed | tf_op | source)
XLA Modules:
  0.0 654.2 jit_solution(5641120072855570488)
XLA Ops:
  8.8 57.7 %scatter_custom_fusion = f32[32768]{0:T(1024)} fusion(s32[8192]{0:T(1024)S(1)} %bitcast.251, f32[8192]{0:T(1024)S(1)} %get-tuple-element.52, f32[]{:T(128)} %constant.82.clone.1), kind=kCustom, calls=%fused_computation.156 | custom fusion | flops 8192 | bytes 131076 | tf_op jit(solution)/shard_map/scatter-add | solution.py:201
  66.5 57.6 %scatter_custom_fusion.1 = f32[32768]{0:T(1024)} fusion(s32[8192]{0:T(1024)S(1)} %bitcast.252, f32[8192]{0:T(1024)S(1)} %get-tuple-element.53, f32[]{:T(128)} %constant.82.clone.1), kind=kCustom, calls=%fused_computation.154 | custom fusion | flops 8192 | bytes 131076 | tf_op jit(solution)/shard_map/scatter-add | solution.py:198
  125.6 4.5 slice.1020
  130.1 4.5 slice.1022
  134.7 4.5 slice.1033
  139.2 4.5 slice.1025
  145.7 236.8 %all-reduce.121.cloned.1.call-done = (f32[32768]{0:T(1024)}, f32[32768]{0:T(1024)}) async-done(((f32[32768]{0:T(1024)}, f32[32768]{0:T(1024)}), (f32[32768]{0:T(1024)}, f32[32768]{0:T(1024)})) %all-reduce.121.cloned.1.call-update) | async-done | bytes 262160
  383.9 4.5 slice.1024
  388.4 4.5 slice.1032
  393.4 4.5 slice.1017
  397.9 4.5 slice.1021
  405.3 3.0 slice.1030
  410.6 3.0 slice.1031
  421.2 3.0 slice.1044
  497.6 8.0 %all-to-all-start.1 = ((f32[8,64,128]{2,0,1:T(8,128)}), f32[8,64,128]{2,0,1:T(8,128)S(1)}, u32[]{:S(2)}, u32[]{:S(2)}) async-start(f32[8,64,128]{2,0,1:T(8,128)} %copy.570), calls=%async_computation.1 | async-start | bytes 524288 | tf_op jit(solution)/shard_map/all_to_all | solution.py:232
  507.4 13.8 %all-to-all-done.1 = f32[8,64,128]{2,0,1:T(8,128)S(1)} async-done(((f32[8,64,128]{2,0,1:T(8,128)}), f32[8,64,128]{2,0,1:T(8,128)S(1)}, u32[]{:S(2)}, u32[]{:S(2)}) %all-to-all-start.1) | async-done | bytes 262176 | tf_op jit(solution)/shard_map/all_to_all | solution.py:232
  521.2 6.2 all-to-all-start.2
  528.3 14.6 %all-to-all-done.2 = f32[8,64,128]{2,0,1:T(8,128)S(1)} async-done(((f32[8,64,128]{2,0,1:T(8,128)}), f32[8,64,128]{2,0,1:T(8,128)S(1)}, u32[]{:S(2)}, u32[]{:S(2)}) %all-to-all-start.2) | async-done | bytes 262176 | tf_op jit(solution)/shard_map/all_to_all | solution.py:231
  542.9 6.4 all-to-all-start
  549.4 15.9 %collective-permute-start = (f32[1,64,128]{2,1,0:T(8,128)S(1)}, f32[1,64,128]{2,1,0:T(8,128)S(1)}, u32[]{:S(2)}, u32[]{:S(2)}) collective-permute-start(f32[1,64,128]{2,1,0:T(8,128)S(1)} %get-tuple-element.98), channel_id=1, source_target_pairs={{0,1},{1,0},{2,3},{3,2},{4,5},{5,4},{6,7},{7,6},{8,9},{9,8},{10,11... | collective-permute-start | bytes 98312 | tf_op jit(solution)/shard_map/ppermute | solution.py:24
  569.0 14.8 %all-to-all-start.3 = ((f32[512,1,128]{2,1,0:T(1,128)}), f32[512,1,128]{2,1,0:T(1,128)S(1)}, u32[]{:S(2)}, u32[]{:S(2)}) async-start(f32[512,1,128]{2,1,0:T(1,128)} %bitcast.85), calls=%async_computation.3 | async-start | bytes 524288 | tf_op jit(solution)/shard_map/all_to_all | solution.py:235
  583.9 3.1 collective-permute-start.1
  587.1 8.0 %collective-permute-start.2 = (f32[1,64,128]{2,1,0:T(8,128)S(1)}, f32[1,64,128]{2,1,0:T(8,128)S(1)}, u32[]{:S(2)}, u32[]{:S(2)}) collective-permute-start(f32[1,64,128]{2,1,0:T(8,128)S(1)} %get-tuple-element.96), channel_id=1, source_target_pairs={{0,3},{1,2},{2,1},{3,0},{4,7},{5,6},{6,5},{7,4},{8,11},{9,10},{10,... | collective-permute-start | bytes 98312 | tf_op jit(solution)/shard_map/ppermute | solution.py:24
  595.1 4.6 collective-permute-start.3
  601.9 3.7 collective-permute-start.5
  605.6 3.3 collective-permute-start.6
  609.1 3.0 collective-permute-done.6
  612.1 4.6 all-to-all-start.5
  618.5 4.8 all-to-all-done.5
  623.3 4.4 all-to-all-start.4
  628.3 5.9 all-to-all-done.4
  636.5 9.9 %all_to_all.108 = f32[1,512,128]{2,0,1:T(1,128)S(1)} all-to-all(f32[1,512,128]{2,0,1:T(1,128)S(1)} %bitcast.220), channel_id=1, replica_groups=mesh['row'=64,'col'=8] {'col'}, dimensions={1} | all-to-all | bytes 524288 | tf_op jit(solution)/shard_map/all_to_all | solution.py:244
  (376 shorter events, 105.2 us)
Async XLA Ops:
  7.2 0.8 copy-start.16
  7.2 375.3 %all-reduce.121.cloned.1.call-start = ((), (), s32[]{:S(2)}) async-start(), calls=%async_computation.7 | async-start | bytes 524288
  7.9 0.8 copy-start.18
  8.8 116.2 %copy-start.11 = (f32[8,64,128]{2,1,0:T(8,128)S(1)}, f32[8,64,128]{2,1,0:T(8,128)}, u32[]{:S(2)}) copy-start(f32[8,64,128]{2,1,0:T(8,128)} %param.17) | copy-start | bytes 786436
  8.8 116.2 %copy-start.15 = (f32[8,64,128]{2,1,0:T(8,128)S(1)}, f32[8,64,128]{2,1,0:T(8,128)}, u32[]{:S(2)}) copy-start(f32[8,64,128]{2,1,0:T(8,128)} %param.16) | copy-start | bytes 786436
  473.1 1.1 copy-start.9
  476.9 1.0 copy-start.10
  479.7 2.0 copy-start.7
  479.7 2.0 copy-start.8
  481.7 4.1 copy-start.5
  481.7 4.1 copy-start.6
  483.8 2.0 copy-start.3
  483.8 2.0 copy-start.4
  487.7 0.9 copy-start.13
  488.7 1.0 copy-start.1
  488.7 1.0 copy-start.2
  488.9 1.0 copy-start
  490.8 0.9 copy-start.14
  493.5 1.0 copy-start.12
  497.6 23.6 %all-to-all-start.1 = ((f32[8,64,128]{2,0,1:T(8,128)}), f32[8,64,128]{2,0,1:T(8,128)S(1)}, u32[]{:S(2)}, u32[]{:S(2)}) async-start(f32[8,64,128]{2,0,1:T(8,128)} %copy.570), calls=%async_computation.1 | async-start | bytes 524288 | tf_op jit(solution)/shard_map/all_to_all | solution.py:232
  521.2 21.7 %all-to-all-start.2 = ((f32[8,64,128]{2,0,1:T(8,128)}), f32[8,64,128]{2,0,1:T(8,128)S(1)}, u32[]{:S(2)}, u32[]{:S(2)}) async-start(f32[8,64,128]{2,0,1:T(8,128)} %copy.571), calls=%async_computation.2 | async-start | bytes 524288 | tf_op jit(solution)/shard_map/all_to_all | solution.py:231
  542.9 23.1 %all-to-all-start = ((f32[8,64,128]{2,0,1:T(8,128)}), f32[8,64,128]{2,0,1:T(8,128)S(1)}, u32[]{:S(2)}, u32[]{:S(2)}) async-start(f32[8,64,128]{2,0,1:T(8,128)} %copy.569), calls=%async_computation | async-start | bytes 524288 | tf_op jit(solution)/shard_map/all_to_all | solution.py:230
  549.4 52.6 %collective-permute-start = (f32[1,64,128]{2,1,0:T(8,128)S(1)}, f32[1,64,128]{2,1,0:T(8,128)S(1)}, u32[]{:S(2)}, u32[]{:S(2)}) collective-permute-start(f32[1,64,128]{2,1,0:T(8,128)S(1)} %get-tuple-element.98), channel_id=1, source_target_pairs={{0,1},{1,0},{2,3},{3,2},{4,5},{5,4},{6,7},{7,6},{8,9},{9,8},{10,11... | collective-permute-start | bytes 98312 | tf_op jit(solution)/shard_map/ppermute | solution.py:24
  569.0 43.1 %all-to-all-start.3 = ((f32[512,1,128]{2,1,0:T(1,128)}), f32[512,1,128]{2,1,0:T(1,128)S(1)}, u32[]{:S(2)}, u32[]{:S(2)}) async-start(f32[512,1,128]{2,1,0:T(1,128)} %bitcast.85), calls=%async_computation.3 | async-start | bytes 524288 | tf_op jit(solution)/shard_map/all_to_all | solution.py:235
  583.9 21.7 %collective-permute-start.1 = (f32[1,64,128]{2,1,0:T(8,128)S(1)}, f32[1,64,128]{2,1,0:T(8,128)S(1)}, u32[]{:S(2)}, u32[]{:S(2)}) collective-permute-start(f32[1,64,128]{2,1,0:T(8,128)S(1)} %get-tuple-element.97), channel_id=1, source_target_pairs={{0,2},{1,3},{2,0},{3,1},{4,6},{5,7},{6,4},{7,5},{8,10},{9,11},{10,... | collective-permute-start | bytes 98312 | tf_op jit(solution)/shard_map/ppermute | solution.py:24
  587.1 21.9 %collective-permute-start.2 = (f32[1,64,128]{2,1,0:T(8,128)S(1)}, f32[1,64,128]{2,1,0:T(8,128)S(1)}, u32[]{:S(2)}, u32[]{:S(2)}) collective-permute-start(f32[1,64,128]{2,1,0:T(8,128)S(1)} %get-tuple-element.96), channel_id=1, source_target_pairs={{0,3},{1,2},{2,1},{3,0},{4,7},{5,6},{6,5},{7,4},{8,11},{9,10},{10,... | collective-permute-start | bytes 98312 | tf_op jit(solution)/shard_map/ppermute | solution.py:24
  595.1 14.0 %collective-permute-start.3 = (f32[1,64,128]{2,1,0:T(8,128)S(1)}, f32[1,64,128]{2,1,0:T(8,128)S(1)}, u32[]{:S(2)}, u32[]{:S(2)}) collective-permute-start(f32[1,64,128]{2,1,0:T(8,128)S(1)} %get-tuple-element.95), channel_id=1, source_target_pairs={{0,4},{1,5},{2,6},{3,7},{4,0},{5,1},{6,2},{7,3},{8,12},{9,13},{10,... | collective-permute-start | bytes 98312 | tf_op jit(solution)/shard_map/ppermute | solution.py:24
  599.7 9.3 %collective-permute-start.4 = (f32[1,64,128]{2,1,0:T(8,128)S(1)}, f32[1,64,128]{2,1,0:T(8,128)S(1)}, u32[]{:S(2)}, u32[]{:S(2)}) collective-permute-start(f32[1,64,128]{2,1,0:T(8,128)S(1)} %get-tuple-element.94), channel_id=1, source_target_pairs={{0,5},{1,4},{2,7},{3,6},{4,1},{5,0},{6,3},{7,2},{8,13},{9,12},{10,... | collective-permute-start | bytes 98312 | tf_op jit(solution)/shard_map/ppermute | solution.py:24
  601.9 7.2 %collective-permute-start.5 = (f32[1,64,128]{2,1,0:T(8,128)S(1)}, f32[1,64,128]{2,1,0:T(8,128)S(1)}, u32[]{:S(2)}, u32[]{:S(2)}) collective-permute-start(f32[1,64,128]{2,1,0:T(8,128)S(1)} %get-tuple-element.93), channel_id=1, source_target_pairs={{0,6},{1,7},{2,4},{3,5},{4,2},{5,3},{6,0},{7,1},{8,14},{9,15},{10,... | collective-permute-start | bytes 98312 | tf_op jit(solution)/shard_map/ppermute | solution.py:24
  605.6 6.4 collective-permute-start.6
  612.1 11.1 %all-to-all-start.5 = ((f32[8,64,128]{2,1,0:T(8,128)}), f32[8,64,128]{2,1,0:T(8,128)S(1)}, u32[]{:S(2)}, u32[]{:S(2)}) async-start(f32[8,64,128]{2,1,0:T(8,128)} %get-tuple-element.171), calls=%async_computation.5 | async-start | bytes 524288 | tf_op jit(solution)/shard_map/all_to_all | solution.py:240
  623.3 10.9 %all-to-all-start.4 = ((f32[8,64,128]{2,1,0:T(8,128)}), f32[8,64,128]{2,1,0:T(8,128)S(1)}, u32[]{:S(2)}, u32[]{:S(2)}) async-start(f32[8,64,128]{2,1,0:T(8,128)} %bitcast_multiply_fusion), calls=%async_computation.4 | async-start | bytes 524288 | tf_op jit(solution)/shard_map/all_to_all | solution.py:239
  (8 other events, 5.7 us)
Sparse Core Ops, SparseCore 0:
  124.3 258.1 all-reduce.120
